TPU v7x, 32 devices: a whole 2x2x4 slice. The times are simulated.
32 devices in a mesh: blk: 8 (over y, x, core), smp: 4 (over z).
Axes of the slice: x: 2, y: 2, z: 4, core: 2. Of those that a mesh axis runs over, the one named last changes fastest.
Arguments:
- field_tiles: bfloat16 [64, 262144], P(None, ('blk', 'smp')), may hold values from -6 to 6
- tile_dest: int32 [2048], replicated, may hold values from 0 to 2047, as said below
- near_cols: int32 [2048, 4], P(('blk', 'smp')), may hold values from 0 to 2047, as said below
- near_tiles: bfloat16 [2048, 4, 128, 128], P(('blk', 'smp')), may hold values from -0.25 to 0.25
- far_left: bfloat16 [5, 64, 262144], P(None, None, ('blk', 'smp')), may hold values from -0.3125 to 0.3125
- far_right: bfloat16 [5, 64, 262144], P(None, None, ('blk', 'smp')), may hold values from -6 to 6
Outputs:
- product: bfloat16 [64, 262144], P(None, ('blk', 'smp'))
Inputs may be any that keep to these rules, and one draw needn't show every extreme that they name: tile_dest is a permutation of the blocks; the tiles of group g go to groups with the same value of g mod 4, exactly 8 of them to each such group. near_cols[b, 0] = b; every other entry lies within 8 of b.
All inputs are finite; a program needn't handle non-finite values.
Results may differ from a plain program's by a relative error of at most 0.0042.
Values may be sent and summed in bfloat16 or wider, within the bound.
A program may use at most 128 MiB of HBM per device.

v0:
```python
import jax
import jax.numpy as jnp
from jax import lax
from jax.sharding import PartitionSpec as P

BLOCK = 128
BPD = 64
RANK = 64
NEAR = 4
REACH = 8
LEVELS = 5


def extended_2(value, sides, width):
    for axis, dim in sides:
        size, length = (lax.axis_size(axis), value.shape[dim])
        up = [(i, (i + 1) % size) for i in range(size - 1)]
        down = [(j, i) for i, j in up]
        last = lax.slice_in_dim(value, length - width, length, axis=dim)
        leading = lax.slice_in_dim(value, 0, width, axis=dim)
        before = lax.ppermute(last, axis, up)
        after = lax.ppermute(leading, axis, down)
        value = jnp.concatenate([before, value, after], axis=dim)
    return value


def shards(field_tiles, tile_dest, near_cols, near_tiles, far_left, far_right):
    samples = field_tiles.shape[0]
    n_blk = lax.axis_size("blk")
    n_smp = lax.axis_size("smp")
    devices = lax.axis_size(("blk", "smp"))
    top_bits = devices.bit_length() - 1
    peer = BPD // n_blk
    my_index = lax.axis_index(("blk", "smp"))
    my_blk = lax.axis_index("blk")
    my_smp = lax.axis_index("smp")
    tile_rows = field_tiles.reshape(samples, BPD, BLOCK)
    own_dest = lax.dynamic_slice_in_dim(tile_dest, my_index * BPD, BPD)
    send_order = jnp.argsort(own_dest // BPD // n_smp, stable=True)
    outgoing = jnp.take(tile_rows, send_order, axis=1).reshape(samples, n_blk, peer, BLOCK)
    arrived = lax.all_to_all(outgoing, "blk", split_axis=1, concat_axis=1, tiled=True)
    source_ids = jnp.arange(n_blk, dtype=jnp.int32) * n_smp + my_smp
    source_dest = jnp.take(tile_dest.reshape(devices, BPD), source_ids, axis=0)
    matches = source_dest // BPD // n_smp == my_blk
    slot_keys = jnp.where(matches, jnp.arange(BPD, dtype=jnp.int32)[None, :], BPD)
    chosen = jnp.sort(slot_keys, axis=1)[:, :peer]
    slots = jnp.take_along_axis(source_dest, chosen, axis=1) % BPD
    inverse = jnp.argsort(slots.reshape(-1))
    hilbert = jnp.take(arrived.reshape(samples, BPD, BLOCK), inverse, axis=1).reshape(
        samples, BPD * BLOCK
    )
    extended = extended_2(hilbert, ((("blk", "smp"), 1),), REACH * BLOCK)
    extended = extended.reshape(samples, BPD + 2 * REACH, BLOCK)
    local_cols = (near_cols - my_index * BPD + REACH).reshape(-1)
    picked = jnp.take(extended, local_cols, axis=1).reshape(samples, BPD, NEAR, BLOCK)
    near_part = jnp.einsum("sbkq,bkpq->sbp", picked, near_tiles, preferred_element_type=jnp.float32)
    near_part = near_part.reshape(samples, BPD * BLOCK)
    projections = jnp.einsum("lrp,sp->lrs", far_right, hilbert, preferred_element_type=jnp.float32)
    level_bits = [top_bits - 1 - level for level in range(LEVELS)]
    every_group = lax.all_gather(projections, ("blk", "smp"), axis=0, tiled=True)
    every_group = every_group.reshape(devices, LEVELS, RANK, samples)
    group_ids = jnp.arange(devices, dtype=jnp.int32)
    bit_column = jnp.array(level_bits, jnp.int32)[:, None]
    wanted = jnp.bitwise_xor(jnp.right_shift(my_index, bit_column), 1)
    level_mask = (jnp.right_shift(group_ids[None, :], bit_column) == wanted).astype(jnp.float32)
    siblings = jnp.einsum("lj,jlrs->lrs", level_mask, every_group, precision=lax.Precision.HIGHEST)
    level_scale = jnp.array(
        [(float(devices >> level + 1) * BPD * BLOCK) ** (-0.5) for level in range(LEVELS)],
        jnp.float32,
    )
    coupling = (siblings * level_scale[:, None, None]).astype(jnp.bfloat16)
    far_part = jnp.einsum("lrp,lrs->sp", far_left, coupling, preferred_element_type=jnp.float32)
    return (near_part + far_part).astype(jnp.bfloat16)


def solution(mesh):
    return jax.shard_map(
        shards,
        mesh=mesh,
        in_specs=(
            P(None, ("blk", "smp")),
            P(),
            P(("blk", "smp"), None),
            P(("blk", "smp"), None, None, None),
            P(None, None, ("blk", "smp")),
            P(None, None, ("blk", "smp")),
        ),
        out_specs=P(None, ("blk", "smp")),
        check_vma=False,
    )
```

profile of v0, /device:TPU:0, one launch (start us, length us, event | category | flops | bytes accessed | tf_op | source)
XLA Modules:
  0.0 126.8 jit_solution(4253213510572984323)
XLA Ops:
  6.5 0.9 and_select_fusion.2
  7.4 2.0 %sort.49 = (s32[64]{0:T(128)}, s32[64]{0:T(128)S(1)}) sort(s32[64]{0:T(128)S(1)} %and_select_fusion.2, s32[64]{0:T(128)S(1)} %iota.25), dimensions={0}, to_apply=%region_0.1 | sort | flops 384 | bytes 1024 | tf_op jit(solution)/shard_map/jit(argsort)/sort | solution.py:39
  9.8 0.8 gather_fusion.3
  10.5 1.1 broadcast_select_fusion.1
  11.7 5.2 %all-to-all-start = ((bf16[64,8,8,128]{3,0,2,1:T(8,128)(2,1)}), bf16[64,8,8,128]{3,0,2,1:T(8,128)(2,1)S(1)}, u32[]{:S(2)}, u32[]{:S(2)}) async-start(bf16[64,8,8,128]{3,0,2,1:T(8,128)(2,1)} %bitcast.3), calls=%async_computation | async-start | bytes 2097152 | tf_op jit(solution)/shard_map/all_to_all | solution.py:41
  17.8 1.0 sort.50
  20.0 2.1 %sort.51 = (s32[64]{0:T(128)}, s32[64]{0:T(128)S(1)}) sort(s32[64]{0:T(128)S(1)} %and_select_fusion.1, s32[64]{0:T(128)S(1)} %iota.29), dimensions={0}, to_apply=%region_2.4 | sort | flops 384 | bytes 1024 | tf_op jit(solution)/shard_map/jit(argsort)/sort | solution.py:48
  22.2 10.1 %all-to-all-done = bf16[64,8,8,128]{3,0,2,1:T(8,128)(2,1)S(1)} async-done(((bf16[64,8,8,128]{3,0,2,1:T(8,128)(2,1)}), bf16[64,8,8,128]{3,0,2,1:T(8,128)(2,1)S(1)}, u32[]{:S(2)}, u32[]{:S(2)}) %all-to-all-start) | async-done | bytes 1048608 | tf_op jit(solution)/shard_map/all_to_all | solution.py:41
  32.3 0.8 gather_fusion.4
  33.0 1.2 fusion.12
  34.2 1.7 %copy.34 = bf16[64,64,128]{2,1,0:T(8,128)(2,1)} copy(bf16[64,64,128]{2,0,1:T(8,128)(2,1)S(1)} %get-tuple-element.15) | data formatting | bytes 2097152 | tf_op jit(solution)/shard_map/jit(_take)/select_n | solution.py:49
  35.9 1.6 %reshape.172 = bf16[64,8192,1]{1,0,2:T(8,128)(2,1)S(1)} reshape(bf16[64,64,128]{2,1,0:T(8,128)(2,1)} %copy.34) | data formatting | bytes 2097152 | tf_op jit(solution)/shard_map/reshape | solution.py:49
  37.5 4.8 %convolution_bitcast_fusion.1 = f32[5,64,64]{1,2,0:T(8,128)S(1)} fusion(bf16[64,8192,1]{1,0,2:T(8,128)(2,1)S(1)} %reshape.172, bf16[5,64,8192]{2,1,0:T(8,128)(2,1)} %param.15), kind=kOutput, calls=%fused_computation.17 | convolution fusion | flops 335544320 | bytes 6373376 | tf_op jit(solution)/shard_map/lrp,sp->lrs/dot_general | solution.py:58
  42.3 0.8 copy.38
  43.7 3.5 %collective-permute-start = (bf16[64,1024]{1,0:T(8,128)(2,1)S(1)}, bf16[64,1024]{1,0:T(8,128)(2,1)S(1)}, u32[]{:S(2)}, u32[]{:S(2)}) collective-permute-start(bf16[64,1024]{1,0:T(8,128)(2,1)S(1)} %get-tuple-element.17), channel_id=1, source_target_pairs={{0,1},{1,2},{2,3},{3,4},{4,5},{5,6},{6,7},{7,8},{8,9},{9,10},{10,1... | collective-permute-start | bytes 393224 | tf_op jit(solution)/shard_map/ppermute | solution.py:21
  47.2 1.5 %collective-permute-start.1 = (bf16[64,1024]{1,0:T(8,128)(2,1)S(1)}, bf16[64,1024]{1,0:T(8,128)(2,1)}, u32[]{:S(2)}, u32[]{:S(2)}) collective-permute-start(bf16[64,1024]{1,0:T(8,128)(2,1)S(1)} %get-tuple-element.18), channel_id=1, source_target_pairs={{1,0},{2,1},{3,2},{4,3},{5,4},{6,5},{7,6},{8,7},{9,8},{10,9},{11,1... | collective-permute-start | bytes 393224 | tf_op jit(solution)/shard_map/ppermute | solution.py:22
  48.8 0.9 collective-permute-done
  49.7 5.6 %collective-permute-done.1 = bf16[64,1024]{1,0:T(8,128)(2,1)} collective-permute-done((bf16[64,1024]{1,0:T(8,128)(2,1)S(1)}, bf16[64,1024]{1,0:T(8,128)(2,1)}, u32[]{:S(2)}, u32[]{:S(2)}) %collective-permute-start.1) | collective-permute-done | bytes 131104 | tf_op jit(solution)/shard_map/ppermute | solution.py:22
  55.3 1.3 copy_bitcast_fusion
  56.5 3.1 %gather_fusion.1 = bf16[256,64,128]{2,1,0:T(8,128)(2,1)} fusion(bf16[64,80,128]{2,0,1:T(8,128)(2,1)S(1)} %copy_bitcast_fusion, s32[1024]{0:T(1024)S(1)} %pad_clamp_fusion), kind=kCustom, calls=%fused_computation.3 | custom fusion | bytes 8389632 | tf_op jit(solution)/shard_map/jit(_take)/gather | solution.py:55
  59.6 7.7 %fusion.8 = f32[64,8,8,128]{3,2,1,0:T(8,128)S(1)} fusion(bf16[64,4,128,128]{3,2,1,0:T(8,128)(2,1)} %param.13, bf16[64,64,4,128]{3,0,2,1:T(8,128)(2,1)} %bitcast.59, pred[64,4]{1,0:T(8,128)(4,1)S(1)} %copy.28), kind=kOutput, calls=%fused_computation.14 | convolution fusion | flops 538968064 | bytes 14680320 | tf_op jit(solution)/shard_map/sbkq,bkpq->sbp/dot_general | solution.py:56
  67.4 40.8 %all-gather.2.cloned.1.call-done = f32[160,64,64]{2,1,0:T(8,128)} async-done(((f32[5,64,64]{2,1,0:T(8,128)}), f32[160,64,64]{2,1,0:T(8,128)}) %all-gather.2.cloned.1.call-update) | async-done | bytes 2621456 | tf_op jit(solution)/shard_map/all_gather | solution.py:60
  108.1 7.0 %fusion.2 = f32[5,1,64,64]{3,1,2,0:T(1,128)S(1)} fusion(f32[32,5,64,64]{3,2,1,0:T(8,128)} %bitcast.62, pred[5,32,1,1]{1,0,2,3:T(8,128)(4,1)S(1)} %fusion.22), kind=kOutput, calls=%fused_computation.8 | convolution fusion | flops 7864320 | bytes 2703520 | tf_op jit(solution)/shard_map/lj,jlrs->lrs/dot_general | solution.py:66
  115.2 4.7 %fusion.1 = bf16[64,8192]{1,0:T(8,128)(2,1)} fusion(bf16[5,64,8192]{2,1,0:T(8,128)(2,1)} %param.14, f32[64,8,8,128]{3,2,1,0:T(8,128)S(1)} %fusion.8, f32[5,1,64,64]{2,3,0,1:T(8,128)S(1)} %copy.42, f32[5]{0:T(128)S(1)} %copy-done.4), kind=kOutput, calls=%fused_computation.7 | convolution fusion | flops 336633856 | bytes 8470548 | tf_op jit(solution)/shard_map/lrp,lrs->sp/dot_general | solution.py:72
  (54 shorter events, 3.2 us)
Async XLA Ops:
  6.5 2.9 %copy-start = (bf16[64,8192]{1,0:T(8,128)(2,1)S(1)}, bf16[64,8192]{1,0:T(8,128)(2,1)}, u32[]{:S(2)}) copy-start(bf16[64,8192]{1,0:T(8,128)(2,1)} %param.10) | copy-start | bytes 3145732
  9.5 7.4 %copy-start.2 = (s32[2048]{0:T(1024)S(1)}, s32[2048]{0:T(1024)}, u32[]{:S(2)}) copy-start(s32[2048]{0:T(1024)} %param.11) | copy-start | bytes 24580
  11.7 20.6 %all-to-all-start = ((bf16[64,8,8,128]{3,0,2,1:T(8,128)(2,1)}), bf16[64,8,8,128]{3,0,2,1:T(8,128)(2,1)S(1)}, u32[]{:S(2)}, u32[]{:S(2)}) async-start(bf16[64,8,8,128]{3,0,2,1:T(8,128)(2,1)} %bitcast.3), calls=%async_computation | async-start | bytes 2097152 | tf_op jit(solution)/shard_map/all_to_all | solution.py:41
  16.9 91.3 %all-gather.2.cloned.1.call-start = ((), (), s32[]{:S(2)}) async-start(), calls=%async_computation.1 | async-start | bytes 5406720 | tf_op jit(solution)/shard_map/all_gather | solution.py:60
  35.9 7.3 %copy-start.3 = (s32[64,4]{0,1:T(4,128)S(1)}, s32[64,4]{0,1:T(4,128)}, u32[]{:S(2)}) copy-start(s32[64,4]{0,1:T(4,128)} %param.12) | copy-start | bytes 3076
  35.9 7.5 %copy-start.5 = (s32[5]{0:T(128)S(1)}, s32[5]{0:T(128)}, u32[]{:S(2)}) copy-start(s32[5]{0:T(128)} %constant.130.clone) | copy-start | bytes 64
  35.9 7.6 %copy-start.1 = (bf16[64,8,8,128]{3,2,1,0:T(8,128)(2,1)S(1)}, bf16[64,8,8,128]{3,2,1,0:T(8,128)(2,1)}, u32[]{:S(2)}) copy-start(bf16[64,8,8,128]{3,2,1,0:T(8,128)(2,1)} %get-tuple-element.16) | copy-start | bytes 3145732
  43.7 6.0 %collective-permute-start = (bf16[64,1024]{1,0:T(8,128)(2,1)S(1)}, bf16[64,1024]{1,0:T(8,128)(2,1)S(1)}, u32[]{:S(2)}, u32[]{:S(2)}) collective-permute-start(bf16[64,1024]{1,0:T(8,128)(2,1)S(1)} %get-tuple-element.17), channel_id=1, source_target_pairs={{0,1},{1,2},{2,3},{3,4},{4,5},{5,6},{6,7},{7,8},{8,9},{9,10},{10,1... | collective-permute-start | bytes 393224 | tf_op jit(solution)/shard_map/ppermute | solution.py:21
  47.2 8.1 %collective-permute-start.1 = (bf16[64,1024]{1,0:T(8,128)(2,1)S(1)}, bf16[64,1024]{1,0:T(8,128)(2,1)}, u32[]{:S(2)}, u32[]{:S(2)}) collective-permute-start(bf16[64,1024]{1,0:T(8,128)(2,1)S(1)} %get-tuple-element.18), channel_id=1, source_target_pairs={{1,0},{2,1},{3,2},{4,3},{5,4},{6,5},{7,6},{8,7},{9,8},{10,9},{11,1... | collective-permute-start | bytes 393224 | tf_op jit(solution)/shard_map/ppermute | solution.py:22
  67.4 47.9 %copy-start.4 = (f32[5]{0:T(128)S(1)}, f32[5]{0:T(128)}, u32[]{:S(2)}) copy-start(f32[5]{0:T(128)} %constant.131.clone) | copy-start | bytes 64
Sparse Core Ops, SparseCore 0:
  43.2 64.8 all-gather.1
where the time goes:
time: 127 us
  waiting for transfers between devices  57.4 us (45%)
  matrix products  24.2 us (19%)
  between operations  13.6 us (11%)
  local copies, waits for them, and re-layouts  11.5 us (9%)
  starting transfers between devices  10.2 us (8%)
  other arithmetic  9.89 us (8%)
    all_gather x1, waiting for transfers between devices, shards(): lax.all_gather(projections, ('blk', 'smp'), axis=0, tiled=True)  40.8 us
    all_to_all x1, waiting for transfers between devices, shards(): lax.all_to_all(outgoing, 'blk', split_axis=1, concat_axis=1, tiled=True)  10.1 us
    dot_general x1, matrix products, shards(): jnp.einsum('sbkq,bkpq->sbp', picked, near_tiles, preferred_element_type=j...  7.71 us
    dot_general x1, matrix products, shards(): jnp.einsum('lj,jlrs->lrs', level_mask, every_group, precision=lax.Precisi...  6.97 us
    ppermute x1, waiting for transfers between devices, extended_2(): after = lax.ppermute(leading, axis, down)  5.58 us
    all_to_all x1, starting transfers between devices, shards(): lax.all_to_all(outgoing, 'blk', split_axis=1, concat_axis=1, tiled=True)  5.17 us
    dot_general x1, matrix products, shards(): jnp.einsum('lrp,sp->lrs', far_right, hilbert, preferred_element_type=jnp....  4.82 us
    dot_general x1, matrix products, shards(): jnp.einsum('lrp,lrs->sp', far_left, coupling, preferred_element_type=jnp....  4.71 us
  transfers between devices with their start and end apart: 4, of which 4 were waited for; matrix products, arithmetic and copies ran while one was open for 14% of the time, Pallas kernels for 0%

commit v1 on v0

v1 whole, which is shorter than its diff:
```python
import functools

import jax
import jax.numpy as jnp
from jax import lax
from jax.experimental import pallas as pl
from jax.experimental.pallas import tpu as pltpu
from jax.sharding import PartitionSpec as P

BLOCK = 128
BPD = 64
RANK = 64
NEAR = 4
REACH = 8
LEVELS = 5
PARTS = 2
MESH = pl.DeviceIdType.MESH
F32 = jnp.float32
BF16 = jnp.bfloat16
NT = (((1,), (1,)), ((), ()))
NN = (((1,), (0,)), ((), ()))


def flipped(value, mask):
    bit = 1
    while bit <= mask:
        if mask & bit:
            value = value + bit - 2 * bit * ((value // bit) % 2)
        bit *= 2
    return value


def halves_swapped(x):
    return pltpu.roll(x, 64, 1)


def kernel(
    n_blk, n_smp, samples,
    field_h, dest_h, cols_h, near_h, left_h, right_h, out_h,
    field_v, tiles_v, near_v, left_v, right_v, dest_v, source_v, order_v, place_v,
    order_s, place_s, cols_s, acc, out_v, proj,
    *rest,
):
    per = samples // PARTS
    half = per // 2
    peer = BPD // n_blk
    blk_bits = n_blk.bit_length() - 1
    smp_levels = LEVELS - blk_bits
    points = BPD * BLOCK
    rest = list(rest)

    def take(n):
        got = rest[:n]
        del rest[:n]
        return got

    outgoing, arrived, hil, low, high = (take(PARTS) for _ in range(5))
    z_send, z_recv, b_send, b_recv = (take(PARTS) for _ in range(4))
    load_sem, a2a_send, a2a_recv, halo_send, halo_recv = take(5)
    zs_sem, zr_sem, bs_sem, br_sem, out_sem = take(5)

    blk = lax.axis_index("blk")
    smp = lax.axis_index("smp")
    me = blk * n_smp + smp

    def load(src, dst, at):
        copy = pltpu.make_async_copy(src, dst, load_sem.at[at])
        copy.start()
        return copy

    dest_load = load(dest_h, dest_v, 0)
    field_load = load(field_h, field_v, 1)
    cols_load = load(cols_h, cols_s, 2)

    following = ((blk + (smp + 1) // n_smp) % n_blk, (smp + 1) % n_smp)
    previous = (
        (blk + n_blk - 1 + (smp + n_smp - 1) // n_smp) % n_blk,
        (smp + n_smp - 1) % n_smp,
    )
    blk_peers = [(flipped(blk, j), smp) for j in range(1, n_blk)]
    smp_peers = [(blk, flipped(smp, j)) for j in range(1, n_smp)]
    everyone = blk_peers + smp_peers + [following, previous]
    barrier = pltpu.get_barrier_semaphore()
    for device in everyone:
        pl.semaphore_signal(barrier, inc=1, device_id=device, device_id_type=MESH)

    right_load = load(right_h, right_v, 3)
    near_load = load(near_h, near_v, 4)
    left_load = load(left_h, left_v, 5)

    rows = lax.broadcasted_iota(jnp.int32, (BPD, 128), 0)
    lanes = lax.broadcasted_iota(jnp.int32, (BPD, 128), 1)
    dest_load.wait()
    own = jnp.broadcast_to(dest_v[pl.ds(me, 1), :], (BPD, 128))
    target = lax.shift_right_arithmetic(own, (BPD * n_smp).bit_length() - 1)
    column = jnp.sum(jnp.where(rows == lanes, target, 0), axis=1, keepdims=True)
    before = jnp.where((target == column) & (lanes < rows), 1, 0)
    place = column * peer + jnp.sum(before, axis=1, keepdims=True)
    order = jnp.sum(jnp.where(place == lanes, rows, 0), axis=0, keepdims=True)
    order_v[...] = jnp.broadcast_to(order, (8, 128))
    order_copy = pltpu.make_async_copy(order_v, order_s, load_sem.at[6])
    order_copy.start()
    field_load.wait()

    def split(t, carry):
        at = pl.multiple_of(t * BLOCK, BLOCK)
        tiles_v[t] = field_v[:, pl.ds(at, BLOCK)]
        return carry

    lax.fori_loop(0, BPD, split, 0, unroll=8)
    order_copy.wait()

    def fill(part, j):
        group = flipped(blk, j)
        into = arrived[part] if j == 0 else outgoing[part]

        def body(i, carry):
            at = group * peer + i
            into[at] = tiles_v[order_s[0, at], pl.ds(part * per, per), :]
            return carry

        lax.fori_loop(0, peer, body, 0, unroll=True)

    def a2a(part, j):
        theirs = flipped(blk, j)
        return pltpu.make_async_remote_copy(
            src_ref=outgoing[part].at[pl.ds(theirs * peer, peer)],
            dst_ref=arrived[part].at[pl.ds(blk * peer, peer)],
            send_sem=a2a_send.at[part, j],
            recv_sem=a2a_recv.at[part, j],
            device_id=(theirs, smp),
            device_id_type=MESH,
        )

    sends = list(range(n_blk - 1, 0, -1))
    for at, j in enumerate(sends):
        fill(0, j)
        if at == 0:
            pl.semaphore_wait(barrier, len(everyone))
        a2a(0, j).start()
    for part in range(PARTS):
        fill(part, 0)
    for part in range(1, PARTS):
        for j in sends:
            fill(part, j)

    for s in range(n_blk):
        source_v[pl.ds(s, 1), :] = dest_v[pl.ds(s * n_smp + smp, 1), :]
    here = source_v[...] - me * BPD
    s_rows = lax.broadcasted_iota(jnp.int32, (n_blk, 128), 0)
    s_lanes = lax.broadcasted_iota(jnp.int32, (n_blk, 128), 1)
    mine = jnp.where((here >= 0) & (here < BPD), 1, 0)
    total = mine
    shift = 1
    while shift < BPD:
        total = total + jnp.where(s_lanes >= shift, pltpu.roll(total, shift, 1), 0)
        shift *= 2
    lands = s_rows * peer + total - mine
    found = jnp.zeros((BPD, 128), jnp.int32)
    for s in range(n_blk):
        found = found + jnp.where(here[s : s + 1, :] == rows, lands[s : s + 1, :], 0)
    found = jnp.sum(found, axis=1, keepdims=True)
    found = jnp.sum(jnp.where(rows == lanes, found, 0), axis=0, keepdims=True)
    found = jnp.minimum(jnp.maximum(found, 0), BPD - 1)
    place_v[...] = jnp.broadcast_to(found, (8, 128))
    place_copy = pltpu.make_async_copy(place_v, place_s, load_sem.at[7])
    place_copy.start()
    place_copy.wait()
    cols_load.wait()

    lane = lax.broadcasted_iota(jnp.int32, (per, 128), 1) < 64
    lane_half = lax.broadcasted_iota(jnp.int32, (half, 128), 1) < 64

    def halo(part, up):
        source = hil[part].at[pl.ds(BPD - REACH, REACH) if up else pl.ds(0, REACH)]
        target_ref = low[part].at[pl.ds(0, REACH)] if up else high[part].at[pl.ds(2 * REACH, REACH)]
        return pltpu.make_async_remote_copy(
            src_ref=source,
            dst_ref=target_ref,
            send_sem=halo_send.at[part, int(up)],
            recv_sem=halo_recv.at[part, int(up)],
            device_id=following if up else previous,
            device_id_type=MESH,
        )

    def z_kind(j):
        return 1 if smp_levels and j == 1 else 0

    def z_copy(part, j):
        return pltpu.make_async_remote_copy(
            src_ref=z_send[part].at[z_kind(j)],
            dst_ref=z_recv[part].at[j],
            send_sem=zs_sem.at[part, j],
            recv_sem=zr_sem.at[part, j],
            device_id=(blk, flipped(smp, j)),
            device_id_type=MESH,
        )

    def b_level(j):
        return blk_bits - j.bit_length()

    def b_copy(part, j):
        return pltpu.make_async_remote_copy(
            src_ref=b_send[part].at[b_level(j)],
            dst_ref=b_recv[part].at[j],
            send_sem=bs_sem.at[part, j],
            recv_sem=br_sem.at[part, j],
            device_id=(flipped(blk, j), smp),
            device_id_type=MESH,
        )

    def gather(part):
        for j in sends:
            a2a(part, j).wait_recv()

        def edge(b, carry):
            first = arrived[part][place_s[0, b]]
            hil[part][b] = first
            low[part][b + REACH] = first
            final = arrived[part][place_s[0, b + BPD - 2 * REACH]]
            hil[part][b + BPD - 2 * REACH] = final
            high[part][b] = final
            return carry

        lax.fori_loop(0, 2 * REACH, edge, 0, unroll=4)
        halo(part, True).start()
        halo(part, False).start()

        def middle(b, carry):
            hil[part][b] = arrived[part][place_s[0, b]]
            return carry

        lax.fori_loop(2 * REACH, BPD - 2 * REACH, middle, 0, unroll=4)

    def project(part):
        proj[...] = jnp.zeros_like(proj)
        group = 8

        def step(i, carry):
            b = i * group
            block = jnp.concatenate([hil[part][b + k] for k in range(group)], axis=1)
            at = pl.multiple_of(i * group * BLOCK, group * BLOCK)
            proj[0 : LEVELS * RANK, 0:per] += lax.dot_general(
                right_v[:, pl.ds(at, group * BLOCK)], block, NT, preferred_element_type=F32
            )
            return carry

        lax.fori_loop(0, BPD // group, step, 0)
        sums = proj[...].T[0:per, :]
        tiles = [sums[:, k * 128 : (k + 1) * 128] for k in range(3)]
        if smp_levels:
            other = jnp.where(lane, tiles[1], halves_swapped(tiles[2]))
            z_send[part][0] = jnp.concatenate(tiles[:2], axis=1).astype(BF16)
            z_send[part][1] = jnp.concatenate([tiles[0], other], axis=1).astype(BF16)
        else:
            z_send[part][0] = sums.astype(BF16)
        for j in range(n_smp - 1, 0, -1):
            z_copy(part, j).start()
        return tiles

    def packed(x, level):
        top, bottom = x[0:half], x[half:per]
        if level % 2 == 0:
            return jnp.where(lane_half, top, halves_swapped(bottom))
        return jnp.where(lane_half, halves_swapped(top), bottom)

    def unpacked(x, level):
        if level % 2 == 0:
            return jnp.concatenate([x, halves_swapped(x)], axis=0)
        return jnp.concatenate([halves_swapped(x), x], axis=0)

    def reduce_smp(part, tiles):
        for j in range(1, n_smp):
            z_copy(part, j).wait_recv()
        got = {j: z_recv[part][j].astype(F32) for j in range(1, n_smp)}
        for level in range(blk_bits):
            t = level // 2
            if level % 2 == 0:
                summed = tiles[t]
                for j in range(1, n_smp):
                    summed = summed + got[j][:, t * 128 : (t + 1) * 128]
            b_send[part][level] = packed(summed, level).astype(BF16)
        for j in sends:
            b_copy(part, j).start()
        if not smp_levels:
            return None
        return got[1][:, 128:256], got[2][:, 128:256] + got[3][:, 128:256]

    def couple(part, inner):
        for j in sends:
            b_copy(part, j).wait_recv()
        by_level = []
        for level in range(blk_bits):
            total = None
            for j in range(1, n_blk):
                if b_level(j) == level:
                    one = b_recv[part][j].astype(F32)
                    total = one if total is None else total + one
            by_level.append(unpacked(total, level))
        if smp_levels:
            by_level.append(inner[1])
            by_level.append(halves_swapped(inner[0]))
        devices = n_blk * n_smp
        scales = [(float(devices >> level + 1) * points) ** -0.5 for level in range(LEVELS)]
        by_level = [x * s for x, s in zip(by_level, scales)]
        first = jnp.where(lane, by_level[0], by_level[1]).astype(BF16)
        second = jnp.where(lane, by_level[2], by_level[3]).astype(BF16)
        third = by_level[4].astype(BF16)[:, 0:RANK]
        return jnp.concatenate([first, second], axis=1), third

    def near_rows(part, source, start, stop):
        def body(b, carry):
            picks = []
            for k in range(NEAR):
                picks.append(source[cols_s[b * NEAR + k]])
            picked = jnp.concatenate(picks, axis=1)
            tile = jnp.concatenate([near_v[b, k] for k in range(NEAR)], axis=1)
            acc[pl.ds(part * per, per), pl.ds(pl.multiple_of(b * BLOCK, BLOCK), BLOCK)] = (
                lax.dot_general(picked, tile, NT, preferred_element_type=F32)
            )
            return carry

        lax.fori_loop(start, stop, body, 0, unroll=4)

    wide = 512
    pieces = 4

    def out_copy(part, piece):
        where = (pl.ds(part * per, per), pl.ds(piece * (points // pieces), points // pieces))
        return pltpu.make_async_copy(out_v.at[where], out_h.at[where], out_sem.at[part, piece])

    def far(part, coupling):
        first, last = coupling

        def body(i, carry):
            at = pl.ds(pl.multiple_of(i * wide, wide), wide)
            value = lax.dot_general(
                first, left_v[0 : 4 * RANK, at], NN, preferred_element_type=F32
            ) + lax.dot_general(
                last, left_v[4 * RANK : 5 * RANK, at], NN, preferred_element_type=F32
            )
            mine = pl.ds(part * per, per)
            out_v[mine, at] = (acc[mine, at] + value).astype(BF16)
            return carry

        for piece in range(pieces):
            steps = points // pieces // wide
            lax.fori_loop(piece * steps, (piece + 1) * steps, body, 0, unroll=2)
            out_copy(part, piece).start()

    for part in range(PARTS):
        gather(part)
        if part + 1 < PARTS:
            for j in sends:
                a2a(part, j).wait_send()
                a2a(part + 1, j).start()
        if part == 0:
            right_load.wait()
        tiles = project(part)
        if part == 0:
            near_load.wait()
        middle_row = BPD // 2
        near_rows(part, hil[part], REACH, middle_row)
        inner = reduce_smp(part, tiles)
        near_rows(part, hil[part], middle_row, BPD - REACH)
        halo(part, True).wait_recv()
        halo(part, False).wait_recv()
        near_rows(part, low[part], 0, REACH)
        near_rows(part, high[part], BPD - REACH, BPD)
        if part == 0:
            left_load.wait()
        far(part, couple(part, inner))

    for j in sends:
        a2a(PARTS - 1, j).wait_send()
    for part in range(PARTS):
        halo(part, True).wait_send()
        halo(part, False).wait_send()
        for j in range(1, n_smp):
            z_copy(part, j).wait_send()
        for j in sends:
            b_copy(part, j).wait_send()
        for piece in range(pieces):
            out_copy(part, piece).wait()


def shards(field_tiles, tile_dest, near_cols, near_tiles, far_left, far_right):
    samples, points = field_tiles.shape
    n_blk = lax.axis_size("blk")
    n_smp = lax.axis_size("smp")
    devices = n_blk * n_smp
    per = samples // PARTS
    blk_bits = n_blk.bit_length() - 1
    smp_levels = LEVELS - blk_bits
    z_wide = 256 if smp_levels else 384
    dest = jnp.pad(tile_dest.reshape(devices, BPD), ((0, 0), (0, 128 - BPD)), constant_values=-1)
    me = lax.axis_index("blk") * n_smp + lax.axis_index("smp")
    row = jnp.arange(BPD, dtype=jnp.int32)[:, None]
    base = jnp.where(row < REACH, -REACH, jnp.where(row < BPD - REACH, 0, BPD - 2 * REACH))
    most = jnp.where((row < REACH) | (row >= BPD - REACH), 3 * REACH, BPD) - 1
    cols = jnp.clip(near_cols - me * BPD - base, 0, most).reshape(-1)
    vmem = pltpu.VMEM
    dma = pltpu.SemaphoreType.DMA
    scratch = [
        vmem((samples, points), BF16),
        vmem((BPD, samples, BLOCK), BF16),
        vmem((BPD, NEAR, BLOCK, BLOCK), BF16),
        vmem((LEVELS * RANK, points), BF16),
        vmem((LEVELS * RANK, points), BF16),
        vmem((devices, 128), jnp.int32),
        vmem((n_blk, 128), jnp.int32),
        vmem((8, 128), jnp.int32),
        vmem((8, 128), jnp.int32),
        pltpu.SMEM((8, 128), jnp.int32),
        pltpu.SMEM((8, 128), jnp.int32),
        pltpu.SMEM((BPD * NEAR,), jnp.int32),
        vmem((samples, points), F32),
        vmem((samples, points), BF16),
        vmem((384, 128), F32),
    ]
    scratch += [vmem((BPD, per, BLOCK), BF16) for _ in range(3 * PARTS)]
    scratch += [vmem((3 * REACH, per, BLOCK), BF16) for _ in range(2 * PARTS)]
    scratch += [vmem((2, per, z_wide), BF16) for _ in range(PARTS)]
    scratch += [vmem((n_smp, per, z_wide), BF16) for _ in range(PARTS)]
    scratch += [vmem((blk_bits, per // 2, 128), BF16) for _ in range(PARTS)]
    scratch += [vmem((n_blk, per // 2, 128), BF16) for _ in range(PARTS)]
    scratch += [
        dma((8,)),
        dma((PARTS, n_blk)), dma((PARTS, n_blk)),
        dma((PARTS, 2)), dma((PARTS, 2)),
        dma((PARTS, n_smp)), dma((PARTS, n_smp)),
        dma((PARTS, n_blk)), dma((PARTS, n_blk)),
        dma((PARTS, 4)),
    ]
    anywhere = pl.BlockSpec(memory_space=pl.ANY)
    return pl.pallas_call(
        functools.partial(kernel, n_blk, n_smp, samples),
        out_shape=jax.ShapeDtypeStruct((samples, points), BF16),
        in_specs=[anywhere] * 6,
        out_specs=anywhere,
        scratch_shapes=scratch,
        compiler_params=pltpu.CompilerParams(
            collective_id=0, has_side_effects=True, vmem_limit_bytes=48 * 1024 * 1024
        ),
        cost_estimate=pl.CostEstimate(
            flops=1_300_000_000, bytes_accessed=22_000_000, transcendentals=0
        ),
    )(
        field_tiles,
        dest,
        cols,
        near_tiles,
        far_left.reshape(LEVELS * RANK, points),
        far_right.reshape(LEVELS * RANK, points),
    )


def solution(mesh):
    return jax.shard_map(
        shards,
        mesh=mesh,
        in_specs=(
            P(None, ("blk", "smp")),
            P(),
            P(("blk", "smp"), None),
            P(("blk", "smp"), None, None, None),
            P(None, None, ("blk", "smp")),
            P(None, None, ("blk", "smp")),
        ),
        out_specs=P(None, ("blk", "smp")),
        check_vma=False,
    )
```

time: 127 us -> 42.4 us (0.33)
  waiting for transfers between devices: 57.4 us -> 0 us
  Pallas kernels: 0 us -> 38.3 us
  matrix products: 24.2 us -> 0 us
  between operations: 13.6 us -> 0.02 us
  starting transfers between devices: 10.2 us -> 0 us
  other arithmetic: 9.89 us -> 0.69 us
  local copies, waits for them, and re-layouts: 11.5 us -> 3.17 us
    all_gather x1 -> x0, waiting for transfers between devices: 40.8 us -> none  [shards(): lax.all_gather(projections, ('blk', 'smp'), axis=0, tiled=True)]
    pallas_call x0 -> x1, Pallas kernels: none -> 38.3 us  [shards(): pl.pallas_call(functools.partial(kernel, n_blk, n_smp, samples), out_shap...]
    dot_general x4 -> x0, matrix products: 24.2 us -> none  [the longest x1 7.71 us: shards(): jnp.einsum('sbkq,bkpq->sbp', picked, near_tiles, preferred_element_type=j...]
    all_to_all x1 -> x0, waiting for transfers between devices: 10.1 us -> none  [shards(): lax.all_to_all(outgoing, 'blk', split_axis=1, concat_axis=1, tiled=True)]
    ppermute x2 -> x0, waiting for transfers between devices: 6.46 us -> none  [the longest x1 5.58 us: extended_2(): after = lax.ppermute(leading, axis, down)]
    gather x9 -> x0, local copies, waits for them, and re-layouts: 6.2 us -> none  [the longest x1 3.11 us: shards(): jnp.take(extended, local_cols, axis=1).reshape(samples, BPD, NEAR, BLOCK)]
    all_to_all x1 -> x0, starting transfers between devices: 5.17 us -> none  [shards(): lax.all_to_all(outgoing, 'blk', split_axis=1, concat_axis=1, tiled=True)]
    sort x3 -> x0, other arithmetic: 5.16 us -> none  [the longest x1 2.12 us: shards(): inverse = jnp.argsort(slots.reshape(-1))]
  transfers between devices with their start and end apart: 4 -> 0, of which waited for: 4 -> 0; matrix products, arithmetic and copies ran while one was open for 14% -> 0% of each run, Pallas kernels for 0% -> 0%
where the time goes in v1:
time: 42.4 us; the launch traced here: 42.2 us
  Pallas kernels  38.3 us (90%)
  local copies, waits for them, and re-layouts  3.17 us (7%)
  other arithmetic  0.69 us (2%)
    pallas_call x1, Pallas kernels, shards(): pl.pallas_call(functools.partial(kernel, n_blk, n_smp, samples), out_shap...  38.3 us
    unnamed x3, local copies, waits for them, and re-layouts  2.19 us

profile of v1, /device:TPU:0, one launch (start us, length us, event | category | flops | bytes accessed | tf_op | source)
XLA Modules:
  0.0 42.2 jit_solution(16525330521321227385)
XLA Ops:
  0.0 0.7 %maximum_minimum_fusion = s32[64,4]{0,1:T(4,128)S(1)} fusion(s32[64,4]{0,1:T(4,128)} %param.8, s32[64]{0:T(128)S(1)} %get-tuple-element.5, s32[]{:T(128)S(6)} %mul.7, s32[64]{0:T(128)S(1)} %get-tuple-element.6), kind=kLoop, calls=%fused_computation | loop fusion | flops 1024 | bytes 2564 | tf_op jit(solution)/shard_map/jit(clip)/min | solution.py:401
  0.7 0.8 %reshape.36 = s32[32,64]{1,0:T(8,128)S(1)} reshape(s32[2048]{0:T(1024)} %param.7) | data formatting | bytes 16384 | tf_op jit(solution)/shard_map/reshape | solution.py:396
  1.5 0.1 copy.7
  1.6 0.1 reshape.37.cols_h
  1.7 0.0 copy-start
  1.7 1.2 %copy-done = bf16[64,8192]{1,0:T(8,128)(2,1)S(1)} copy-done((bf16[64,8192]{1,0:T(8,128)(2,1)S(1)}, bf16[64,8192]{1,0:T(8,128)(2,1)}, u32[]{:S(2)}) %copy-start) | copy-done | bytes 1048600
  2.9 38.3 %shard_map.64 = bf16[64,8192]{1,0:T(8,128)(2,1)S(1)} custom-call(bf16[64,8192]{1,0:T(8,128)(2,1)S(1)} %copy-done, s32[32,128]{1,0:T(8,128)S(1)} %pad.4.dest_h, s32[256]{0:T(256)S(1)} %reshape.37.cols_h, bf16[64,4,128,128]{3,2,1,0:T(8,128)(2,1)} %near_h.1, bf16[320,8192]{1,0:T(8,128)(2,1)} %bitcast.2, bf16[320,8192]{1,0:T(8,128)(2,1)} %bitcast.3), custom_call_target="tpu_custom_call" | custom-call | flops 1300000000 | bytes 22000000 | tf_op jit(solution)/shard_map/pallas_call | solution.py:436
  41.2 1.0 %copy.9 = bf16[64,8192]{1,0:T(8,128)(2,1)} copy(bf16[64,8192]{1,0:T(8,128)(2,1)S(1)} %shard_map.64) | data formatting | bytes 2097152
  (2 shorter events, 0.0 us)
Async XLA Ops:
  1.7 1.2 %copy-start = (bf16[64,8192]{1,0:T(8,128)(2,1)S(1)}, bf16[64,8192]{1,0:T(8,128)(2,1)}, u32[]{:S(2)}) copy-start(bf16[64,8192]{1,0:T(8,128)(2,1)} %field_h.1) | copy-start | bytes 3145732

commit v2 on v1

--- a/solution.py
+++ b/solution.py
@@ -37,8 +37,8 @@
 def kernel(
     n_blk, n_smp, samples,
     field_h, dest_h, cols_h, near_h, left_h, right_h, out_h,
-    field_v, tiles_v, near_v, left_v, right_v, dest_v, source_v, order_v, place_v,
-    order_s, place_s, cols_s, acc, out_v, proj,
+    field_v, tiles_v, near_v, left_v, right_v, dest_v, cols_v, source_v, order_v, place_v,
+    order_s, place_s, acc, out_v, proj,
     *rest,
 ):
     per = samples // PARTS
@@ -70,7 +70,7 @@
 
     dest_load = load(dest_h, dest_v, 0)
     field_load = load(field_h, field_v, 1)
-    cols_load = load(cols_h, cols_s, 2)
+    cols_load = load(cols_h, cols_v, 2)
 
     following = ((blk + (smp + 1) // n_smp) % n_blk, (smp + 1) % n_smp)
     previous = (
@@ -91,7 +91,8 @@
     rows = lax.broadcasted_iota(jnp.int32, (BPD, 128), 0)
     lanes = lax.broadcasted_iota(jnp.int32, (BPD, 128), 1)
     dest_load.wait()
-    own = jnp.broadcast_to(dest_v[pl.ds(me, 1), :], (BPD, 128))
+    own = jnp.broadcast_to(dest_v[pl.ds(me // 2, 1), :], (BPD, 128))
+    own = jnp.where(lanes < BPD, pltpu.roll(own, 64 * (me % 2), 1), -1)
     target = lax.shift_right_arithmetic(own, (BPD * n_smp).bit_length() - 1)
     column = jnp.sum(jnp.where(rows == lanes, target, 0), axis=1, keepdims=True)
     before = jnp.where((target == column) & (lanes < rows), 1, 0)
@@ -145,10 +146,11 @@
             fill(part, j)
 
     for s in range(n_blk):
-        source_v[pl.ds(s, 1), :] = dest_v[pl.ds(s * n_smp + smp, 1), :]
-    here = source_v[...] - me * BPD
+        source_v[pl.ds(s, 1), :] = dest_v[pl.ds((s * n_smp + smp) // 2, 1), :]
+    here = pltpu.roll(source_v[...], 64 * (smp % 2), 1) - me * BPD
     s_rows = lax.broadcasted_iota(jnp.int32, (n_blk, 128), 0)
     s_lanes = lax.broadcasted_iota(jnp.int32, (n_blk, 128), 1)
+    here = jnp.where(s_lanes < BPD, here, -1)
     mine = jnp.where((here >= 0) & (here < BPD), 1, 0)
     total = mine
     shift = 1
@@ -163,10 +165,15 @@
     found = jnp.sum(jnp.where(rows == lanes, found, 0), axis=0, keepdims=True)
     found = jnp.minimum(jnp.maximum(found, 0), BPD - 1)
     place_v[...] = jnp.broadcast_to(found, (8, 128))
+    cols_load.wait()
+    c_lanes = lax.broadcasted_iota(jnp.int32, (NEAR, BPD), 1)
+    inner_row = (c_lanes >= REACH) & (c_lanes < BPD - REACH)
+    base = jnp.where(inner_row, 0, jnp.where(c_lanes < REACH, -REACH, BPD - 2 * REACH))
+    most = jnp.where(inner_row, BPD, 3 * REACH) - 1
+    place_v[0:NEAR, 0:BPD] = jnp.minimum(jnp.maximum(cols_v[...] - me * BPD - base, 0), most)
     place_copy = pltpu.make_async_copy(place_v, place_s, load_sem.at[7])
     place_copy.start()
     place_copy.wait()
-    cols_load.wait()
 
     lane = lax.broadcasted_iota(jnp.int32, (per, 128), 1) < 64
     lane_half = lax.broadcasted_iota(jnp.int32, (half, 128), 1) < 64
@@ -210,14 +217,11 @@
         )
 
     def gather(part):
-        for j in sends:
-            a2a(part, j).wait_recv()
-
         def edge(b, carry):
-            first = arrived[part][place_s[0, b]]
+            first = arrived[part][place_s[NEAR, b]]
             hil[part][b] = first
             low[part][b + REACH] = first
-            final = arrived[part][place_s[0, b + BPD - 2 * REACH]]
+            final = arrived[part][place_s[NEAR, b + BPD - 2 * REACH]]
             hil[part][b + BPD - 2 * REACH] = final
             high[part][b] = final
             return carry
@@ -227,7 +231,7 @@
         halo(part, False).start()
 
         def middle(b, carry):
-            hil[part][b] = arrived[part][place_s[0, b]]
+            hil[part][b] = arrived[part][place_s[NEAR, b]]
             return carry
 
         lax.fori_loop(2 * REACH, BPD - 2 * REACH, middle, 0, unroll=4)
@@ -308,15 +312,16 @@
         third = by_level[4].astype(BF16)[:, 0:RANK]
         return jnp.concatenate([first, second], axis=1), third
 
-    def near_rows(part, source, start, stop):
+    def near_rows(sources, start, stop):
         def body(b, carry):
             picks = []
             for k in range(NEAR):
-                picks.append(source[cols_s[b * NEAR + k]])
+                at = place_s[k, b]
+                picks.append(jnp.concatenate([source[at] for source in sources], axis=0))
             picked = jnp.concatenate(picks, axis=1)
             tile = jnp.concatenate([near_v[b, k] for k in range(NEAR)], axis=1)
-            acc[pl.ds(part * per, per), pl.ds(pl.multiple_of(b * BLOCK, BLOCK), BLOCK)] = (
-                lax.dot_general(picked, tile, NT, preferred_element_type=F32)
+            acc[:, pl.ds(pl.multiple_of(b * BLOCK, BLOCK), BLOCK)] = lax.dot_general(
+                picked, tile, NT, preferred_element_type=F32
             )
             return carry
 
@@ -325,12 +330,13 @@
     wide = 512
     pieces = 4
 
-    def out_copy(part, piece):
-        where = (pl.ds(part * per, per), pl.ds(piece * (points // pieces), points // pieces))
-        return pltpu.make_async_copy(out_v.at[where], out_h.at[where], out_sem.at[part, piece])
-
-    def far(part, coupling):
-        first, last = coupling
+    def out_copy(piece):
+        where = (slice(None), pl.ds(piece * (points // pieces), points // pieces))
+        return pltpu.make_async_copy(out_v.at[where], out_h.at[where], out_sem.at[piece])
+
+    def far(couplings):
+        first = jnp.concatenate([c[0] for c in couplings], axis=0)
+        last = jnp.concatenate([c[1] for c in couplings], axis=0)
 
         def body(i, carry):
             at = pl.ds(pl.multiple_of(i * wide, wide), wide)
@@ -339,37 +345,41 @@
             ) + lax.dot_general(
                 last, left_v[4 * RANK : 5 * RANK, at], NN, preferred_element_type=F32
             )
-            mine = pl.ds(part * per, per)
-            out_v[mine, at] = (acc[mine, at] + value).astype(BF16)
+            out_v[:, at] = (acc[:, at] + value).astype(BF16)
             return carry
 
         for piece in range(pieces):
             steps = points // pieces // wide
             lax.fori_loop(piece * steps, (piece + 1) * steps, body, 0, unroll=2)
-            out_copy(part, piece).start()
-
+            out_copy(piece).start()
+
+    tiles = [None] * PARTS
+    inner = [None] * PARTS
     for part in range(PARTS):
-        gather(part)
         if part + 1 < PARTS:
             for j in sends:
                 a2a(part, j).wait_send()
                 a2a(part + 1, j).start()
+        for j in sends:
+            a2a(part, j).wait_recv()
+        gather(part)
         if part == 0:
             right_load.wait()
-        tiles = project(part)
-        if part == 0:
-            near_load.wait()
-        middle_row = BPD // 2
-        near_rows(part, hil[part], REACH, middle_row)
-        inner = reduce_smp(part, tiles)
-        near_rows(part, hil[part], middle_row, BPD - REACH)
+        tiles[part] = project(part)
+        if part > 0:
+            inner[part - 1] = reduce_smp(part - 1, tiles[part - 1])
+    near_load.wait()
+    middle_row = BPD // 2
+    near_rows(hil, REACH, middle_row)
+    inner[PARTS - 1] = reduce_smp(PARTS - 1, tiles[PARTS - 1])
+    near_rows(hil, middle_row, BPD - REACH)
+    for part in range(PARTS):
         halo(part, True).wait_recv()
         halo(part, False).wait_recv()
-        near_rows(part, low[part], 0, REACH)
-        near_rows(part, high[part], BPD - REACH, BPD)
-        if part == 0:
-            left_load.wait()
-        far(part, couple(part, inner))
+    near_rows(low, 0, REACH)
+    near_rows(high, BPD - REACH, BPD)
+    left_load.wait()
+    far([couple(part, inner[part]) for part in range(PARTS)])
 
     for j in sends:
         a2a(PARTS - 1, j).wait_send()
@@ -380,8 +390,8 @@
             z_copy(part, j).wait_send()
         for j in sends:
             b_copy(part, j).wait_send()
-        for piece in range(pieces):
-            out_copy(part, piece).wait()
+    for piece in range(pieces):
+        out_copy(piece).wait()
 
 
 def shards(field_tiles, tile_dest, near_cols, near_tiles, far_left, far_right):
@@ -393,12 +403,6 @@
     blk_bits = n_blk.bit_length() - 1
     smp_levels = LEVELS - blk_bits
     z_wide = 256 if smp_levels else 384
-    dest = jnp.pad(tile_dest.reshape(devices, BPD), ((0, 0), (0, 128 - BPD)), constant_values=-1)
-    me = lax.axis_index("blk") * n_smp + lax.axis_index("smp")
-    row = jnp.arange(BPD, dtype=jnp.int32)[:, None]
-    base = jnp.where(row < REACH, -REACH, jnp.where(row < BPD - REACH, 0, BPD - 2 * REACH))
-    most = jnp.where((row < REACH) | (row >= BPD - REACH), 3 * REACH, BPD) - 1
-    cols = jnp.clip(near_cols - me * BPD - base, 0, most).reshape(-1)
     vmem = pltpu.VMEM
     dma = pltpu.SemaphoreType.DMA
     scratch = [
@@ -407,13 +411,13 @@
         vmem((BPD, NEAR, BLOCK, BLOCK), BF16),
         vmem((LEVELS * RANK, points), BF16),
         vmem((LEVELS * RANK, points), BF16),
-        vmem((devices, 128), jnp.int32),
+        vmem((devices * BPD // 128, 128), jnp.int32),
+        vmem((NEAR, BPD), jnp.int32),
         vmem((n_blk, 128), jnp.int32),
         vmem((8, 128), jnp.int32),
         vmem((8, 128), jnp.int32),
         pltpu.SMEM((8, 128), jnp.int32),
         pltpu.SMEM((8, 128), jnp.int32),
-        pltpu.SMEM((BPD * NEAR,), jnp.int32),
         vmem((samples, points), F32),
         vmem((samples, points), BF16),
         vmem((384, 128), F32),
@@ -430,7 +434,7 @@
         dma((PARTS, 2)), dma((PARTS, 2)),
         dma((PARTS, n_smp)), dma((PARTS, n_smp)),
         dma((PARTS, n_blk)), dma((PARTS, n_blk)),
-        dma((PARTS, 4)),
+        dma((4,)),
     ]
     anywhere = pl.BlockSpec(memory_space=pl.ANY)
     return pl.pallas_call(
@@ -440,15 +444,15 @@
         out_specs=anywhere,
         scratch_shapes=scratch,
         compiler_params=pltpu.CompilerParams(
-            collective_id=0, has_side_effects=True, vmem_limit_bytes=48 * 1024 * 1024
+            collective_id=0, has_side_effects=True, vmem_limit_bytes=60 * 1024 * 1024
         ),
         cost_estimate=pl.CostEstimate(
             flops=1_300_000_000, bytes_accessed=22_000_000, transcendentals=0
         ),
     )(
         field_tiles,
-        dest,
-        cols,
+        tile_dest.reshape(devices * BPD // 128, 128),
+        near_cols.T,
         near_tiles,
         far_left.reshape(LEVELS * RANK, points),
         far_right.reshape(LEVELS * RANK, points),

time: 42.4 us -> 34.4 us (0.81)
  Pallas kernels: 38.3 us -> 31.9 us
  local copies, waits for them, and re-layouts: 3.17 us -> 2.26 us
  other arithmetic: 0.69 us -> 0 us
    pallas_call x1, Pallas kernels: 38.3 us -> 31.9 us  [shards(): pl.pallas_call(functools.partial(kernel, n_blk, n_smp, samples), out_shap...]
    reshape x2 -> x0, local copies, waits for them, and re-layouts: 0.87 us -> none  [the longest x1 0.77 us: shards(): tile_dest.reshape(devices, BPD)]
    min x1 -> x0, other arithmetic: 0.69 us -> none  [shards(): cols = jnp.clip(near_cols - me * BPD - base, 0, most).reshape(-1)]
    unnamed x3 -> x1, local copies, waits for them, and re-layouts: 2.19 us -> 2.26 us
where the time goes in v2:
time: 34.4 us; the launch traced here: 34.2 us
  Pallas kernels  31.9 us (93%)
  local copies, waits for them, and re-layouts  2.26 us (7%)
    pallas_call x1, Pallas kernels, shards(): pl.pallas_call(functools.partial(kernel, n_blk, n_smp, samples), out_shap...  31.9 us
    unnamed x1, local copies, waits for them, and re-layouts  2.26 us

profile of v2, /device:TPU:0, one launch (start us, length us, event | category | flops | bytes accessed | tf_op | source)
XLA Modules:
  0.0 34.2 jit_solution(10736933065098796855)
XLA Ops:
  0.0 31.9 %shard_map.64 = bf16[64,8192]{1,0:T(8,128)(2,1)} custom-call(bf16[64,8192]{1,0:T(8,128)(2,1)} %field_h.1, s32[16,128]{1,0:T(8,128)} %bitcast.6, s32[4,64]{1,0:T(4,128)} %bitcast.7, bf16[64,4,128,128]{3,2,1,0:T(8,128)(2,1)} %near_h.1, bf16[320,8192]{1,0:T(8,128)(2,1)} %bitcast.4, bf16[320,8192]{1,0:T(8,128)(2,1)} %bitcast.5), custom_call_target="tpu_custom_call" | custom-call | flops 1300000000 | bytes 22000000 | tf_op jit(solution)/shard_map/pallas_call | solution.py:440
  31.9 2.3 %copy.8 = bf16[64,8192]{1,0:T(8,128)(2,1)} copy(bf16[64,8192]{1,0:T(8,128)(2,1)} %shard_map.64) | data formatting | bytes 2097152

commit v3 on v2

--- a/solution.py
+++ b/solution.py
@@ -36,9 +36,9 @@
 
 def kernel(
     n_blk, n_smp, samples,
-    field_h, dest_h, cols_h, near_h, left_h, right_h, out_h,
+    field_h, dest_h, cols_h, near_h, left_h, right_h, out_ref,
     field_v, tiles_v, near_v, left_v, right_v, dest_v, cols_v, source_v, order_v, place_v,
-    order_s, place_s, acc, out_v, proj,
+    order_s, place_s, acc, proj,
     *rest,
 ):
     per = samples // PARTS
@@ -57,7 +57,7 @@
     outgoing, arrived, hil, low, high = (take(PARTS) for _ in range(5))
     z_send, z_recv, b_send, b_recv = (take(PARTS) for _ in range(4))
     load_sem, a2a_send, a2a_recv, halo_send, halo_recv = take(5)
-    zs_sem, zr_sem, bs_sem, br_sem, out_sem = take(5)
+    zs_sem, zr_sem, bs_sem, br_sem = take(4)
 
     blk = lax.axis_index("blk")
     smp = lax.axis_index("smp")
@@ -84,9 +84,16 @@
     for device in everyone:
         pl.semaphore_signal(barrier, inc=1, device_id=device, device_id_type=MESH)
 
-    right_load = load(right_h, right_v, 3)
-    near_load = load(near_h, near_v, 4)
-    left_load = load(left_h, left_v, 5)
+    def load_parts(src, dst, at, parts):
+        size = src.shape[0] // parts
+        for i in range(parts):
+            rows_i = pl.ds(i * size, size)
+            load(src.at[rows_i], dst.at[rows_i], at)
+        return pltpu.make_async_copy(src, dst, load_sem.at[at])
+
+    right_load = load_parts(right_h, right_v, 3, 10)
+    near_load = load_parts(near_h, near_v, 4, 16)
+    left_load = load_parts(left_h, left_v, 5, 10)
 
     rows = lax.broadcasted_iota(jnp.int32, (BPD, 128), 0)
     lanes = lax.broadcasted_iota(jnp.int32, (BPD, 128), 1)
@@ -328,12 +335,6 @@
         lax.fori_loop(start, stop, body, 0, unroll=4)
 
     wide = 512
-    pieces = 4
-
-    def out_copy(piece):
-        where = (slice(None), pl.ds(piece * (points // pieces), points // pieces))
-        return pltpu.make_async_copy(out_v.at[where], out_h.at[where], out_sem.at[piece])
-
     def far(couplings):
         first = jnp.concatenate([c[0] for c in couplings], axis=0)
         last = jnp.concatenate([c[1] for c in couplings], axis=0)
@@ -345,13 +346,10 @@
             ) + lax.dot_general(
                 last, left_v[4 * RANK : 5 * RANK, at], NN, preferred_element_type=F32
             )
-            out_v[:, at] = (acc[:, at] + value).astype(BF16)
-            return carry
-
-        for piece in range(pieces):
-            steps = points // pieces // wide
-            lax.fori_loop(piece * steps, (piece + 1) * steps, body, 0, unroll=2)
-            out_copy(piece).start()
+            out_ref[:, at] = (acc[:, at] + value).astype(BF16)
+            return carry
+
+        lax.fori_loop(0, points // wide, body, 0, unroll=4)
 
     tiles = [None] * PARTS
     inner = [None] * PARTS
@@ -390,8 +388,6 @@
             z_copy(part, j).wait_send()
         for j in sends:
             b_copy(part, j).wait_send()
-    for piece in range(pieces):
-        out_copy(piece).wait()
 
 
 def shards(field_tiles, tile_dest, near_cols, near_tiles, far_left, far_right):
@@ -419,7 +415,6 @@
         pltpu.SMEM((8, 128), jnp.int32),
         pltpu.SMEM((8, 128), jnp.int32),
         vmem((samples, points), F32),
-        vmem((samples, points), BF16),
         vmem((384, 128), F32),
     ]
     scratch += [vmem((BPD, per, BLOCK), BF16) for _ in range(3 * PARTS)]
@@ -434,17 +429,15 @@
         dma((PARTS, 2)), dma((PARTS, 2)),
         dma((PARTS, n_smp)), dma((PARTS, n_smp)),
         dma((PARTS, n_blk)), dma((PARTS, n_blk)),
-        dma((4,)),
     ]
-    anywhere = pl.BlockSpec(memory_space=pl.ANY)
     return pl.pallas_call(
         functools.partial(kernel, n_blk, n_smp, samples),
         out_shape=jax.ShapeDtypeStruct((samples, points), BF16),
-        in_specs=[anywhere] * 6,
-        out_specs=anywhere,
+        in_specs=[pl.BlockSpec(memory_space=pltpu.HBM)] * 6,
+        out_specs=pl.BlockSpec(memory_space=vmem),
         scratch_shapes=scratch,
         compiler_params=pltpu.CompilerParams(
-            collective_id=0, has_side_effects=True, vmem_limit_bytes=60 * 1024 * 1024
+            collective_id=0, has_side_effects=True, vmem_limit_bytes=48 * 1024 * 1024
         ),
         cost_estimate=pl.CostEstimate(
             flops=1_300_000_000, bytes_accessed=22_000_000, transcendentals=0

time: 34.4 us -> 34.8 us (1.012)
  local copies, waits for them, and re-layouts: 2.26 us -> 3.57 us
  Pallas kernels: 31.9 us -> 31 us
    unnamed x1 -> x7, local copies, waits for them, and re-layouts: 2.26 us -> 3.57 us
    pallas_call x1, Pallas kernels: 31.9 us -> 31 us  [shards(): pl.pallas_call(functools.partial(kernel, n_blk, n_smp, samples), out_shap...]
where the time goes in v3:
time: 34.8 us; the launch traced here: 34.6 us
  Pallas kernels  31 us (89%)
  local copies, waits for them, and re-layouts  3.57 us (10%)
    pallas_call x1, Pallas kernels, shards(): pl.pallas_call(functools.partial(kernel, n_blk, n_smp, samples), out_shap...  31 us
    unnamed x7, local copies, waits for them, and re-layouts  3.57 us

profile of v3, /device:TPU:0, one launch (start us, length us, event | category | flops | bytes accessed | tf_op | source)
XLA Modules:
  0.0 34.6 jit_solution(5675858270785230999)
XLA Ops:
  0.0 0.0 copy-start
  0.0 1.2 %copy-done = bf16[64,8192]{1,0:T(8,128)(2,1)S(1)} copy-done((bf16[64,8192]{1,0:T(8,128)(2,1)S(1)}, bf16[64,8192]{1,0:T(8,128)(2,1)}, u32[]{:S(2)}) %copy-start) | copy-done | bytes 1048600
  1.2 0.0 copy-start.1
  1.2 0.7 %copy-done.1 = s32[2048]{0:T(1024)S(1)} copy-done((s32[2048]{0:T(1024)S(1)}, s32[2048]{0:T(1024)}, u32[]{:S(2)}) %copy-start.1) | copy-done | bytes 8216
  1.9 0.0 copy-start.2
  1.9 0.7 %copy-done.2 = s32[64,4]{0,1:T(4,128)S(1)} copy-done((s32[64,4]{0,1:T(4,128)S(1)}, s32[64,4]{0,1:T(4,128)}, u32[]{:S(2)}) %copy-start.2) | copy-done | bytes 1048
  2.6 31.0 %shard_map.64 = bf16[64,8192]{1,0:T(8,128)(2,1)S(1)} custom-call(bf16[64,8192]{1,0:T(8,128)(2,1)S(1)} %copy-done, s32[16,128]{1,0:T(8,128)S(1)} %bitcast.4, s32[4,64]{1,0:T(4,128)S(1)} %bitcast.5, bf16[64,4,128,128]{3,2,1,0:T(8,128)(2,1)} %near_h.1, bf16[320,8192]{1,0:T(8,128)(2,1)} %bitcast.6, bf16[320,8192]{1,0:T(8,128)(2,1)} %bitcast.7), custom_call_target="tpu_custom_call" | custom-call | flops 1300000000 | bytes 22000000 | tf_op jit(solution)/shard_map/pallas_call | solution.py:433
  33.6 1.0 %copy.8 = bf16[64,8192]{1,0:T(8,128)(2,1)} copy(bf16[64,8192]{1,0:T(8,128)(2,1)S(1)} %shard_map.64) | data formatting | bytes 2097152
Async XLA Ops:
  0.0 1.2 %copy-start = (bf16[64,8192]{1,0:T(8,128)(2,1)S(1)}, bf16[64,8192]{1,0:T(8,128)(2,1)}, u32[]{:S(2)}) copy-start(bf16[64,8192]{1,0:T(8,128)(2,1)} %field_h.1) | copy-start | bytes 3145732
  1.2 0.7 %copy-start.1 = (s32[2048]{0:T(1024)S(1)}, s32[2048]{0:T(1024)}, u32[]{:S(2)}) copy-start(s32[2048]{0:T(1024)} %param.7) | copy-start | bytes 24580
  1.9 0.7 %copy-start.2 = (s32[64,4]{0,1:T(4,128)S(1)}, s32[64,4]{0,1:T(4,128)}, u32[]{:S(2)}) copy-start(s32[64,4]{0,1:T(4,128)} %param.8) | copy-start | bytes 3076

commit v4 on v2

--- a/solution.py
+++ b/solution.py
@@ -13,7 +13,7 @@
 NEAR = 4
 REACH = 8
 LEVELS = 5
-PARTS = 2
+PARTS = 1
 MESH = pl.DeviceIdType.MESH
 F32 = jnp.float32
 BF16 = jnp.bfloat16
@@ -84,7 +84,12 @@
     for device in everyone:
         pl.semaphore_signal(barrier, inc=1, device_id=device, device_id_type=MESH)
 
-    right_load = load(right_h, right_v, 3)
+    def right_block(b, carry):
+        at = pl.multiple_of(b * BLOCK, BLOCK)
+        load(right_h.at[:, pl.ds(at, BLOCK)], right_v.at[b], 3)
+        return carry
+
+    lax.fori_loop(0, BPD, right_block, 0)
     near_load = load(near_h, near_v, 4)
     left_load = load(left_h, left_v, 5)
 
@@ -133,17 +138,16 @@
             device_id_type=MESH,
         )
 
-    sends = list(range(n_blk - 1, 0, -1))
+    sends = [j for j in (1, 2, 4, 6, 7, 3, 5) if j < n_blk]
+    sends += [j for j in range(8, n_blk)]
+    window = 4
     for at, j in enumerate(sends):
         fill(0, j)
         if at == 0:
             pl.semaphore_wait(barrier, len(everyone))
-        a2a(0, j).start()
-    for part in range(PARTS):
-        fill(part, 0)
-    for part in range(1, PARTS):
-        for j in sends:
-            fill(part, j)
+        if at < window:
+            a2a(0, j).start()
+    fill(0, 0)
 
     for s in range(n_blk):
         source_v[pl.ds(s, 1), :] = dest_v[pl.ds((s * n_smp + smp) // 2, 1), :]
@@ -158,13 +162,21 @@
         total = total + jnp.where(s_lanes >= shift, pltpu.roll(total, shift, 1), 0)
         shift *= 2
     lands = s_rows * peer + total - mine
+    lands = jnp.where(mine > 0, lands, -1)
     found = jnp.zeros((BPD, 128), jnp.int32)
+    block_of = jnp.zeros((BPD, 128), jnp.int32)
     for s in range(n_blk):
-        found = found + jnp.where(here[s : s + 1, :] == rows, lands[s : s + 1, :], 0)
-    found = jnp.sum(found, axis=1, keepdims=True)
-    found = jnp.sum(jnp.where(rows == lanes, found, 0), axis=0, keepdims=True)
-    found = jnp.minimum(jnp.maximum(found, 0), BPD - 1)
-    place_v[...] = jnp.broadcast_to(found, (8, 128))
+        here_s, lands_s = here[s : s + 1, :], lands[s : s + 1, :]
+        found = found + jnp.where(here_s == rows, lands_s, 0)
+        block_of = block_of + jnp.where(lands_s == rows, here_s, 0)
+
+    def row_of(x):
+        x = jnp.sum(x, axis=1, keepdims=True)
+        x = jnp.sum(jnp.where(rows == lanes, x, 0), axis=0, keepdims=True)
+        return jnp.minimum(jnp.maximum(x, 0), BPD - 1)
+
+    place_v[...] = jnp.broadcast_to(row_of(found), (8, 128))
+    place_v[NEAR + 1 : NEAR + 2, :] = row_of(block_of)
     cols_load.wait()
     c_lanes = lax.broadcasted_iota(jnp.int32, (NEAR, BPD), 1)
     inner_row = (c_lanes >= REACH) & (c_lanes < BPD - REACH)
@@ -236,20 +248,15 @@
 
         lax.fori_loop(2 * REACH, BPD - 2 * REACH, middle, 0, unroll=4)
 
-    def project(part):
-        proj[...] = jnp.zeros_like(proj)
-        group = 8
-
-        def step(i, carry):
-            b = i * group
-            block = jnp.concatenate([hil[part][b + k] for k in range(group)], axis=1)
-            at = pl.multiple_of(i * group * BLOCK, group * BLOCK)
-            proj[0 : LEVELS * RANK, 0:per] += lax.dot_general(
-                right_v[:, pl.ds(at, group * BLOCK)], block, NT, preferred_element_type=F32
-            )
-            return carry
-
-        lax.fori_loop(0, BPD // group, step, 0)
+    def project(part, j):
+        first = flipped(blk, j) * peer
+        wide_rows = [right_v[place_s[NEAR + 1, first + i]] for i in range(peer)]
+        block = jnp.concatenate([arrived[part][first + i] for i in range(peer)], axis=1)
+        proj[0 : LEVELS * RANK, 0:per] += lax.dot_general(
+            jnp.concatenate(wide_rows, axis=1), block, NT, preferred_element_type=F32
+        )
+
+    def send_projections(part):
         sums = proj[...].T[0:per, :]
         tiles = [sums[:, k * 128 : (k + 1) * 128] for k in range(3)]
         if smp_levels:
@@ -283,7 +290,7 @@
                 summed = tiles[t]
                 for j in range(1, n_smp):
                     summed = summed + got[j][:, t * 128 : (t + 1) * 128]
-            b_send[part][level] = packed(summed, level).astype(BF16)
+            b_send[part][level] = packed(summed, level)
         for j in sends:
             b_copy(part, j).start()
         if not smp_levels:
@@ -298,7 +305,7 @@
             total = None
             for j in range(1, n_blk):
                 if b_level(j) == level:
-                    one = b_recv[part][j].astype(F32)
+                    one = b_recv[part][j]
                     total = one if total is None else total + one
             by_level.append(unpacked(total, level))
         if smp_levels:
@@ -355,21 +362,20 @@
 
     tiles = [None] * PARTS
     inner = [None] * PARTS
-    for part in range(PARTS):
-        if part + 1 < PARTS:
-            for j in sends:
-                a2a(part, j).wait_send()
-                a2a(part + 1, j).start()
-        for j in sends:
-            a2a(part, j).wait_recv()
-        gather(part)
-        if part == 0:
-            right_load.wait()
-        tiles[part] = project(part)
-        if part > 0:
-            inner[part - 1] = reduce_smp(part - 1, tiles[part - 1])
+    proj[...] = jnp.zeros_like(proj)
+    pltpu.make_async_copy(right_v, right_v, load_sem.at[3]).wait()
+    project(0, 0)
+    for at, j in enumerate(sends):
+        following_send = at + window - 1
+        if at >= 1 and following_send < len(sends):
+            a2a(0, sends[at]).wait_send()
+            a2a(0, sends[following_send]).start()
+        a2a(0, j).wait_recv()
+        project(0, j)
+    tiles[0] = send_projections(0)
+    gather(0)
     near_load.wait()
-    middle_row = BPD // 2
+    middle_row = BPD * 5 // 8
     near_rows(hil, REACH, middle_row)
     inner[PARTS - 1] = reduce_smp(PARTS - 1, tiles[PARTS - 1])
     near_rows(hil, middle_row, BPD - REACH)
@@ -381,8 +387,9 @@
     left_load.wait()
     far([couple(part, inner[part]) for part in range(PARTS)])
 
-    for j in sends:
-        a2a(PARTS - 1, j).wait_send()
+    for at, j in enumerate(sends):
+        if at < 1 or at + window - 1 >= len(sends):
+            a2a(0, j).wait_send()
     for part in range(PARTS):
         halo(part, True).wait_send()
         halo(part, False).wait_send()
@@ -410,7 +417,7 @@
         vmem((BPD, samples, BLOCK), BF16),
         vmem((BPD, NEAR, BLOCK, BLOCK), BF16),
         vmem((LEVELS * RANK, points), BF16),
-        vmem((LEVELS * RANK, points), BF16),
+        vmem((BPD, LEVELS * RANK, BLOCK), BF16),
         vmem((devices * BPD // 128, 128), jnp.int32),
         vmem((NEAR, BPD), jnp.int32),
         vmem((n_blk, 128), jnp.int32),
@@ -426,8 +433,8 @@
     scratch += [vmem((3 * REACH, per, BLOCK), BF16) for _ in range(2 * PARTS)]
     scratch += [vmem((2, per, z_wide), BF16) for _ in range(PARTS)]
     scratch += [vmem((n_smp, per, z_wide), BF16) for _ in range(PARTS)]
-    scratch += [vmem((blk_bits, per // 2, 128), BF16) for _ in range(PARTS)]
-    scratch += [vmem((n_blk, per // 2, 128), BF16) for _ in range(PARTS)]
+    scratch += [vmem((blk_bits, per // 2, 128), F32) for _ in range(PARTS)]
+    scratch += [vmem((n_blk, per // 2, 128), F32) for _ in range(PARTS)]
     scratch += [
         dma((8,)),
         dma((PARTS, n_blk)), dma((PARTS, n_blk)),

time: 34.4 us -> 36.6 us (1.064)
  Pallas kernels: 31.9 us -> 34.1 us
    pallas_call x1, Pallas kernels: 31.9 us -> 34.1 us  [shards(): pl.pallas_call(functools.partial(kernel, n_blk, n_smp, samples), out_shap...]
where the time goes in v4:
time: 36.6 us; the launch traced here: 36.4 us
  Pallas kernels  34.1 us (93%)
  local copies, waits for them, and re-layouts  2.26 us (6%)
    pallas_call x1, Pallas kernels, shards(): pl.pallas_call(functools.partial(kernel, n_blk, n_smp, samples), out_shap...  34.1 us
    unnamed x1, local copies, waits for them, and re-layouts  2.26 us

profile of v4, /device:TPU:0, one launch (start us, length us, event | category | flops | bytes accessed | tf_op | source)
XLA Modules:
  0.0 36.4 jit_solution(8862714492338415599)
XLA Ops:
  0.0 34.1 %shard_map.64 = bf16[64,8192]{1,0:T(8,128)(2,1)} custom-call(bf16[64,8192]{1,0:T(8,128)(2,1)} %field_h.1, s32[16,128]{1,0:T(8,128)} %bitcast.6, s32[4,64]{1,0:T(4,128)} %bitcast.7, bf16[64,4,128,128]{3,2,1,0:T(8,128)(2,1)} %near_h.1, bf16[320,8192]{1,0:T(8,128)(2,1)} %bitcast.4, bf16[320,8192]{1,0:T(8,128)(2,1)} %bitcast.5), custom_call_target="tpu_custom_call" | custom-call | flops 1300000000 | bytes 22000000 | tf_op jit(solution)/shard_map/pallas_call | solution.py:447
  34.1 2.3 %copy.8 = bf16[64,8192]{1,0:T(8,128)(2,1)} copy(bf16[64,8192]{1,0:T(8,128)(2,1)} %shard_map.64) | data formatting | bytes 2097152

commit v5 on v4

--- a/solution.py
+++ b/solution.py
@@ -13,7 +13,7 @@
 NEAR = 4
 REACH = 8
 LEVELS = 5
-PARTS = 1
+PARTS = 2
 MESH = pl.DeviceIdType.MESH
 F32 = jnp.float32
 BF16 = jnp.bfloat16
@@ -140,14 +140,16 @@
 
     sends = [j for j in (1, 2, 4, 6, 7, 3, 5) if j < n_blk]
     sends += [j for j in range(8, n_blk)]
-    window = 4
-    for at, j in enumerate(sends):
-        fill(0, j)
+    window = 5
+    messages = [(part, j) for part in range(PARTS) for j in sends]
+    for at, (part, j) in enumerate(messages):
+        fill(part, j)
         if at == 0:
             pl.semaphore_wait(barrier, len(everyone))
         if at < window:
-            a2a(0, j).start()
-    fill(0, 0)
+            a2a(part, j).start()
+    for part in range(PARTS):
+        fill(part, 0)
 
     for s in range(n_blk):
         source_v[pl.ds(s, 1), :] = dest_v[pl.ds((s * n_smp + smp) // 2, 1), :]
@@ -332,7 +334,7 @@
             )
             return carry
 
-        lax.fori_loop(start, stop, body, 0, unroll=4)
+        lax.fori_loop(start, stop, body, 0, unroll=8)
 
     wide = 512
     pieces = 4
@@ -365,15 +367,23 @@
     proj[...] = jnp.zeros_like(proj)
     pltpu.make_async_copy(right_v, right_v, load_sem.at[3]).wait()
     project(0, 0)
-    for at, j in enumerate(sends):
-        following_send = at + window - 1
-        if at >= 1 and following_send < len(sends):
-            a2a(0, sends[at]).wait_send()
-            a2a(0, sends[following_send]).start()
-        a2a(0, j).wait_recv()
-        project(0, j)
-    tiles[0] = send_projections(0)
-    gather(0)
+    waited = set()
+    for at, (part, j) in enumerate(messages):
+        later = at + window - 1
+        if at >= 1 and later < len(messages):
+            waited.add(at)
+            a2a(*messages[at]).wait_send()
+            a2a(*messages[later]).start()
+        a2a(part, j).wait_recv()
+        project(part, j)
+        if part > 0 and j == sends[3]:
+            inner[part - 1] = reduce_smp(part - 1, tiles[part - 1])
+        if j == sends[-1]:
+            tiles[part] = send_projections(part)
+            gather(part)
+            if part + 1 < PARTS:
+                proj[...] = jnp.zeros_like(proj)
+                project(part + 1, 0)
     near_load.wait()
     middle_row = BPD * 5 // 8
     near_rows(hil, REACH, middle_row)
@@ -387,9 +397,9 @@
     left_load.wait()
     far([couple(part, inner[part]) for part in range(PARTS)])
 
-    for at, j in enumerate(sends):
-        if at < 1 or at + window - 1 >= len(sends):
-            a2a(0, j).wait_send()
+    for at, message in enumerate(messages):
+        if at not in waited:
+            a2a(*message).wait_send()
     for part in range(PARTS):
         halo(part, True).wait_send()
         halo(part, False).wait_send()

time: 36.6 us -> 34 us (0.929)
  Pallas kernels: 34.1 us -> 31.6 us
    pallas_call x1, Pallas kernels: 34.1 us -> 31.6 us  [shards(): pl.pallas_call(functools.partial(kernel, n_blk, n_smp, samples), out_shap...]
where the time goes in v5:
time: 34 us; the launch traced here: 33.8 us
  Pallas kernels  31.6 us (93%)
  local copies, waits for them, and re-layouts  2.26 us (7%)
    pallas_call x1, Pallas kernels, shards(): pl.pallas_call(functools.partial(kernel, n_blk, n_smp, samples), out_shap...  31.6 us
    unnamed x1, local copies, waits for them, and re-layouts  2.26 us

profile of v5, /device:TPU:0, one launch (start us, length us, event | category | flops | bytes accessed | tf_op | source)
XLA Modules:
  0.0 33.8 jit_solution(5316798783620188065)
XLA Ops:
  0.0 31.6 %shard_map.64 = bf16[64,8192]{1,0:T(8,128)(2,1)} custom-call(bf16[64,8192]{1,0:T(8,128)(2,1)} %field_h.1, s32[16,128]{1,0:T(8,128)} %bitcast.6, s32[4,64]{1,0:T(4,128)} %bitcast.7, bf16[64,4,128,128]{3,2,1,0:T(8,128)(2,1)} %near_h.1, bf16[320,8192]{1,0:T(8,128)(2,1)} %bitcast.4, bf16[320,8192]{1,0:T(8,128)(2,1)} %bitcast.5), custom_call_target="tpu_custom_call" | custom-call | flops 1300000000 | bytes 22000000 | tf_op jit(solution)/shard_map/pallas_call | solution.py:457
  31.6 2.3 %copy.8 = bf16[64,8192]{1,0:T(8,128)(2,1)} copy(bf16[64,8192]{1,0:T(8,128)(2,1)} %shard_map.64) | data formatting | bytes 2097152

commit v6 on v5

--- a/solution.py
+++ b/solution.py
@@ -36,9 +36,9 @@
 
 def kernel(
     n_blk, n_smp, samples,
-    field_h, dest_h, cols_h, near_h, left_h, right_h, out_h,
+    field_h, dest_h, cols_h, near_h, left_h, right_h, out_ref,
     field_v, tiles_v, near_v, left_v, right_v, dest_v, cols_v, source_v, order_v, place_v,
-    order_s, place_s, acc, out_v, proj,
+    order_s, place_s, acc, proj,
     *rest,
 ):
     per = samples // PARTS
@@ -57,7 +57,7 @@
     outgoing, arrived, hil, low, high = (take(PARTS) for _ in range(5))
     z_send, z_recv, b_send, b_recv = (take(PARTS) for _ in range(4))
     load_sem, a2a_send, a2a_recv, halo_send, halo_recv = take(5)
-    zs_sem, zr_sem, bs_sem, br_sem, out_sem = take(5)
+    zs_sem, zr_sem, bs_sem, br_sem = take(4)
 
     blk = lax.axis_index("blk")
     smp = lax.axis_index("smp")
@@ -330,19 +330,13 @@
             picked = jnp.concatenate(picks, axis=1)
             tile = jnp.concatenate([near_v[b, k] for k in range(NEAR)], axis=1)
             acc[:, pl.ds(pl.multiple_of(b * BLOCK, BLOCK), BLOCK)] = lax.dot_general(
-                picked, tile, NT, preferred_element_type=F32
-            )
+                tile, picked, NT, preferred_element_type=F32
+            ).T
             return carry
 
         lax.fori_loop(start, stop, body, 0, unroll=8)
 
     wide = 512
-    pieces = 4
-
-    def out_copy(piece):
-        where = (slice(None), pl.ds(piece * (points // pieces), points // pieces))
-        return pltpu.make_async_copy(out_v.at[where], out_h.at[where], out_sem.at[piece])
-
     def far(couplings):
         first = jnp.concatenate([c[0] for c in couplings], axis=0)
         last = jnp.concatenate([c[1] for c in couplings], axis=0)
@@ -354,13 +348,10 @@
             ) + lax.dot_general(
                 last, left_v[4 * RANK : 5 * RANK, at], NN, preferred_element_type=F32
             )
-            out_v[:, at] = (acc[:, at] + value).astype(BF16)
+            out_ref[:, at] = (acc[:, at] + value).astype(BF16)
             return carry
 
-        for piece in range(pieces):
-            steps = points // pieces // wide
-            lax.fori_loop(piece * steps, (piece + 1) * steps, body, 0, unroll=2)
-            out_copy(piece).start()
+        lax.fori_loop(0, points // wide, body, 0, unroll=4)
 
     tiles = [None] * PARTS
     inner = [None] * PARTS
@@ -407,8 +398,6 @@
             z_copy(part, j).wait_send()
         for j in sends:
             b_copy(part, j).wait_send()
-    for piece in range(pieces):
-        out_copy(piece).wait()
 
 
 def shards(field_tiles, tile_dest, near_cols, near_tiles, far_left, far_right):
@@ -436,7 +425,6 @@
         pltpu.SMEM((8, 128), jnp.int32),
         pltpu.SMEM((8, 128), jnp.int32),
         vmem((samples, points), F32),
-        vmem((samples, points), BF16),
         vmem((384, 128), F32),
     ]
     scratch += [vmem((BPD, per, BLOCK), BF16) for _ in range(3 * PARTS)]
@@ -451,17 +439,16 @@
         dma((PARTS, 2)), dma((PARTS, 2)),
         dma((PARTS, n_smp)), dma((PARTS, n_smp)),
         dma((PARTS, n_blk)), dma((PARTS, n_blk)),
-        dma((4,)),
     ]
     anywhere = pl.BlockSpec(memory_space=pl.ANY)
     return pl.pallas_call(
         functools.partial(kernel, n_blk, n_smp, samples),
         out_shape=jax.ShapeDtypeStruct((samples, points), BF16),
         in_specs=[anywhere] * 6,
-        out_specs=anywhere,
+        out_specs=pl.BlockSpec(memory_space=vmem),
         scratch_shapes=scratch,
         compiler_params=pltpu.CompilerParams(
-            collective_id=0, has_side_effects=True, vmem_limit_bytes=60 * 1024 * 1024
+            collective_id=0, has_side_effects=True, vmem_limit_bytes=52 * 1024 * 1024
         ),
         cost_estimate=pl.CostEstimate(
             flops=1_300_000_000, bytes_accessed=22_000_000, transcendentals=0

time: 34 us -> 33.1 us (0.974)
  Pallas kernels: 31.6 us -> 30.5 us
    pallas_call x1, Pallas kernels: 31.6 us -> 30.5 us  [shards(): pl.pallas_call(functools.partial(kernel, n_blk, n_smp, samples), out_shap...]
    unnamed x1 -> x5, local copies, waits for them, and re-layouts: 2.26 us -> 2.35 us
where the time goes in v6:
time: 33.1 us; the launch traced here: 32.8 us
  Pallas kernels  30.5 us (92%)
  local copies, waits for them, and re-layouts  2.35 us (7%)
    pallas_call x1, Pallas kernels, shards(): pl.pallas_call(functools.partial(kernel, n_blk, n_smp, samples), out_shap...  30.5 us
    unnamed x5, local copies, waits for them, and re-layouts  2.35 us

profile of v6, /device:TPU:0, one launch (start us, length us, event | category | flops | bytes accessed | tf_op | source)
XLA Modules:
  0.0 32.8 jit_solution(1150182341393050)
XLA Ops:
  0.0 0.0 copy-start
  0.0 0.7 %copy-done = s32[2048]{0:T(1024)S(1)} copy-done((s32[2048]{0:T(1024)S(1)}, s32[2048]{0:T(1024)}, u32[]{:S(2)}) %copy-start) | copy-done | bytes 8216
  0.7 0.0 copy-start.1
  0.7 0.7 %copy-done.1 = s32[64,4]{0,1:T(4,128)S(1)} copy-done((s32[64,4]{0,1:T(4,128)S(1)}, s32[64,4]{0,1:T(4,128)}, u32[]{:S(2)}) %copy-start.1) | copy-done | bytes 1048
  1.4 30.5 %shard_map.64 = bf16[64,8192]{1,0:T(8,128)(2,1)S(1)} custom-call(bf16[64,8192]{1,0:T(8,128)(2,1)} %field_h.1, s32[16,128]{1,0:T(8,128)S(1)} %bitcast.4, s32[4,64]{1,0:T(4,128)S(1)} %bitcast.5, bf16[64,4,128,128]{3,2,1,0:T(8,128)(2,1)} %near_h.1, bf16[320,8192]{1,0:T(8,128)(2,1)} %bitcast.6, bf16[320,8192]{1,0:T(8,128)(2,1)} %bitcast.7), custom_call_target="tpu_custom_call" | custom-call | flops 1300000000 | bytes 22000000 | tf_op jit(solution)/shard_map/pallas_call | solution.py:444
  31.9 1.0 %copy.8 = bf16[64,8192]{1,0:T(8,128)(2,1)} copy(bf16[64,8192]{1,0:T(8,128)(2,1)S(1)} %shard_map.64) | data formatting | bytes 2097152
Async XLA Ops:
  0.0 0.7 %copy-start = (s32[2048]{0:T(1024)S(1)}, s32[2048]{0:T(1024)}, u32[]{:S(2)}) copy-start(s32[2048]{0:T(1024)} %param.7) | copy-start | bytes 24580
  0.7 0.7 %copy-start.1 = (s32[64,4]{0,1:T(4,128)S(1)}, s32[64,4]{0,1:T(4,128)}, u32[]{:S(2)}) copy-start(s32[64,4]{0,1:T(4,128)} %param.8) | copy-start | bytes 3076

commit v7 on v6

--- a/solution.py
+++ b/solution.py
@@ -140,7 +140,7 @@
 
     sends = [j for j in (1, 2, 4, 6, 7, 3, 5) if j < n_blk]
     sends += [j for j in range(8, n_blk)]
-    window = 5
+    window = 8
     messages = [(part, j) for part in range(PARTS) for j in sends]
     for at, (part, j) in enumerate(messages):
         fill(part, j)

time: 33.1 us -> 32.3 us (0.976)
  Pallas kernels: 30.5 us -> 29.7 us
    pallas_call x1, Pallas kernels: 30.5 us -> 29.7 us  [shards(): pl.pallas_call(functools.partial(kernel, n_blk, n_smp, samples), out_shap...]
where the time goes in v7:
time: 32.3 us; the launch traced here: 32 us
  Pallas kernels  29.7 us (92%)
  local copies, waits for them, and re-layouts  2.35 us (7%)
    pallas_call x1, Pallas kernels, shards(): pl.pallas_call(functools.partial(kernel, n_blk, n_smp, samples), out_shap...  29.7 us
    unnamed x5, local copies, waits for them, and re-layouts  2.35 us

profile of v7, /device:TPU:0, one launch (start us, length us, event | category | flops | bytes accessed | tf_op | source)
XLA Modules:
  0.0 32.0 jit_solution(9517310658805515709)
XLA Ops:
  0.0 0.0 copy-start
  0.0 0.7 %copy-done = s32[2048]{0:T(1024)S(1)} copy-done((s32[2048]{0:T(1024)S(1)}, s32[2048]{0:T(1024)}, u32[]{:S(2)}) %copy-start) | copy-done | bytes 8216
  0.7 0.0 copy-start.1
  0.7 0.7 %copy-done.1 = s32[64,4]{0,1:T(4,128)S(1)} copy-done((s32[64,4]{0,1:T(4,128)S(1)}, s32[64,4]{0,1:T(4,128)}, u32[]{:S(2)}) %copy-start.1) | copy-done | bytes 1048
  1.4 29.7 %shard_map.64 = bf16[64,8192]{1,0:T(8,128)(2,1)S(1)} custom-call(bf16[64,8192]{1,0:T(8,128)(2,1)} %field_h.1, s32[16,128]{1,0:T(8,128)S(1)} %bitcast.4, s32[4,64]{1,0:T(4,128)S(1)} %bitcast.5, bf16[64,4,128,128]{3,2,1,0:T(8,128)(2,1)} %near_h.1, bf16[320,8192]{1,0:T(8,128)(2,1)} %bitcast.6, bf16[320,8192]{1,0:T(8,128)(2,1)} %bitcast.7), custom_call_target="tpu_custom_call" | custom-call | flops 1300000000 | bytes 22000000 | tf_op jit(solution)/shard_map/pallas_call | solution.py:444
  31.1 1.0 %copy.8 = bf16[64,8192]{1,0:T(8,128)(2,1)} copy(bf16[64,8192]{1,0:T(8,128)(2,1)S(1)} %shard_map.64) | data formatting | bytes 2097152
Async XLA Ops:
  0.0 0.7 %copy-start = (s32[2048]{0:T(1024)S(1)}, s32[2048]{0:T(1024)}, u32[]{:S(2)}) copy-start(s32[2048]{0:T(1024)} %param.7) | copy-start | bytes 24580
  0.7 0.7 %copy-start.1 = (s32[64,4]{0,1:T(4,128)S(1)}, s32[64,4]{0,1:T(4,128)}, u32[]{:S(2)}) copy-start(s32[64,4]{0,1:T(4,128)} %param.8) | copy-start | bytes 3076
